TPU v7x, 512 devices: a whole 4x4x16 slice. The times are simulated.
512 devices in a mesh: ctx: 128 (over y, z_lo, x), tp: 4 (over z_hi, core).
Axes of the slice: x: 4, y: 4, z: 16 (z_hi: 2, z_lo: 8; z = z_hi * 8 + z_lo), core: 2. Of those that a mesh axis runs over, the one named last changes fastest.
Arguments:
- query_proj: bfloat16 [16384, 4096], P('ctx', 'tp'), may hold values from -6 to 6
- key_proj: bfloat16 [16384, 4096], P('ctx', 'tp'), may hold values from -6 to 6
- value_proj: bfloat16 [16384, 4096], P('ctx', 'tp'), may hold values from -6 to 6
- cotangent: bfloat16 [16384, 4096], P('ctx', 'tp'), may hold values from -6 to 6
- filter_taps: float32 [16384, 4096], P('ctx', 'tp'), may hold values from -1 to 1
- short_weights: float32 [3, 3, 4096], P(None, None, 'tp'), may hold values from -3.5 to 3.5
Outputs:
- gated_out: bfloat16 [16384, 4096], P('ctx', 'tp')
- query_grad: bfloat16 [16384, 4096], P('ctx', 'tp')
- key_grad: bfloat16 [16384, 4096], P('ctx', 'tp')
- value_grad: bfloat16 [16384, 4096], P('ctx', 'tp')
- filter_grad: float32 [16384, 4096], P('ctx', 'tp')
- short_grad: float32 [3, 3, 4096], P(None, None, 'tp')
All inputs are finite; a program needn't handle non-finite values.
Results may differ from a plain program's by a relative error of at most 0.0065.
Values may be sent and summed in bfloat16 or wider, within the bound.
A program may use at most 64 MiB of HBM per device.

v0:
```python
import math
import jax
import jax.numpy as jnp
from jax import lax
from jax.sharding import PartitionSpec as P


def from_behind(array, axis, by):
    peers = lax.axis_size(axis)
    pairs = [(i, i + by) for i in range(peers) if 0 <= i + by < peers]
    return lax.ppermute(array, axis, pairs)


def contract(form, left, right):
    return jnp.einsum(
        form, left, right, precision=lax.Precision.HIGHEST, preferred_element_type=jnp.float32
    )


def dft_tables(rows, cols, period):
    row_ids = lax.broadcasted_iota(jnp.int32, (rows, cols), 0)
    col_ids = lax.broadcasted_iota(jnp.int32, (rows, cols), 1)
    angle = 2.0 * math.pi / period * (row_ids * col_ids % period).astype(jnp.float32)
    return (jnp.cos(angle), jnp.sin(angle))


def make_plan(seq_len):
    small_len = int(math.isqrt(2 * seq_len))
    while seq_len % small_len:
        small_len -= 1
    large_len = 2 * seq_len // small_len
    large_cos, large_sin = dft_tables(large_len // 2, large_len, large_len)
    small_cos, small_sin = dft_tables(small_len, small_len, small_len)
    twist_cos, twist_sin = dft_tables(large_len, small_len, small_len * large_len)
    fwd_large = jnp.stack([large_cos, -large_sin], axis=1)
    fwd_small = jnp.stack([jnp.stack([small_cos, -small_sin]), jnp.stack([small_sin, small_cos])])
    inv_small = jnp.stack([jnp.stack([small_cos, small_sin]), jnp.stack([-small_sin, small_cos])])
    inv_large = jnp.stack([large_cos, -large_sin])
    return (small_len, large_len, fwd_large, fwd_small, inv_small, inv_large, twist_cos, twist_sin)


def forward_spec(signal, dft_plan):
    small_len, large_len, fwd_large, fwd_small, inv_small, inv_large, twist_cos, twist_sin = (
        dft_plan
    )
    cube = signal.reshape(signal.shape[0], large_len // 2, small_len)
    section_one = contract("cba,bpk->cpka", cube, fwd_large)
    real_one = section_one[:, 0]
    imag_one = section_one[:, 1]
    section_two = jnp.stack(
        [real_one * twist_cos + imag_one * twist_sin, imag_one * twist_cos - real_one * twist_sin],
        axis=1,
    )
    return contract("cpka,pqaj->cqkj", section_two, fwd_small)


def inverse_half(spec, dft_plan):
    small_len, large_len, fwd_large, fwd_small, inv_small, inv_large, twist_cos, twist_sin = (
        dft_plan
    )
    section_one = contract("cqkj,qpja->cpka", spec, inv_small)
    real_one = section_one[:, 0]
    imag_one = section_one[:, 1]
    section_two = jnp.stack(
        [real_one * twist_cos - imag_one * twist_sin, imag_one * twist_cos + real_one * twist_sin],
        axis=1,
    )
    signal = contract("cpka,pbk->cba", section_two, inv_large)
    return signal.reshape(signal.shape[0], -1) / float(small_len * large_len)


def complex_mul(left, right):
    left_real, left_imag = (left[:, 0], left[:, 1])
    right_real, right_imag = (right[:, 0], right[:, 1])
    return jnp.stack(
        [
            left_real * right_real - left_imag * right_imag,
            left_real * right_imag + left_imag * right_real,
        ],
        axis=1,
    )


def conj_mul(left, right):
    left_real, left_imag = (left[:, 0], left[:, 1])
    right_real, right_imag = (right[:, 0], right[:, 1])
    return jnp.stack(
        [
            left_real * right_real + left_imag * right_imag,
            left_real * right_imag - left_imag * right_real,
        ],
        axis=1,
    )


def conv_forward(prod_chan, filter_spec, dft_plan):
    prod_spec = forward_spec(prod_chan.astype(jnp.float32), dft_plan)
    conv_chan = inverse_half(complex_mul(prod_spec, filter_spec), dft_plan).astype(jnp.bfloat16)
    return (conv_chan, prod_spec)


def conv_backward(grad_chan, filter_spec, prod_spec, dft_plan, grad_scale):
    grad_spec = forward_spec(grad_chan.astype(jnp.float32), dft_plan)
    dconv_chan = inverse_half(conj_mul(filter_spec, grad_spec), dft_plan).astype(jnp.bfloat16)
    dfilter_chan = inverse_half(conj_mul(prod_spec, grad_spec), dft_plan) * grad_scale
    return (dconv_chan, dfilter_chan)


def receive_filter(filter_taps, dft_plan):
    filter_chan = lax.all_to_all(filter_taps.T, "ctx", split_axis=0, concat_axis=1, tiled=True)
    return forward_spec(filter_chan, dft_plan)


def return_filter(dfilter_chan):
    return (
        lax.all_to_all(
            dfilter_chan.astype(jnp.bfloat16), "ctx", split_axis=1, concat_axis=0, tiled=True
        )
        .astype(dfilter_chan.dtype)
        .T
    )


def causal_taps(extended, weights, length, axis):
    rim_rows = len(weights) - 1
    summed = weights[0] * lax.slice_in_dim(extended, rim_rows, rim_rows + length, axis=axis)
    for offset in range(1, len(weights)):
        summed = summed + weights[offset] * lax.slice_in_dim(
            extended, rim_rows - offset, rim_rows - offset + length, axis=axis
        )
    return summed


def reverse_taps(extended, weights, length, axis):
    summed = weights[0] * lax.slice_in_dim(extended, 0, length, axis=axis)
    for offset in range(1, len(weights)):
        summed = summed + weights[offset] * lax.slice_in_dim(
            extended, offset, offset + length, axis=axis
        )
    return summed


def tap_grads(grad_in, extended, tap_count, length, axis):
    rim_rows = tap_count - 1
    rows = [
        jnp.sum(
            grad_in
            * lax.slice_in_dim(extended, rim_rows - offset, rim_rows - offset + length, axis=axis),
            axis=axis,
        )
        for offset in range(tap_count)
    ]
    return jnp.stack(rows, axis=1)


def shards(query_proj, key_proj, value_proj, cotangent, filter_taps, short_weights):
    tokens = query_proj.shape[0]
    tap_count = short_weights.shape[1]
    rim_rows = tap_count - 1
    seq_len = tokens * lax.axis_size("ctx")
    grad_scale = 1.0 / math.sqrt(seq_len)
    dft_plan = make_plan(seq_len)
    stacked = jnp.stack([query_proj, key_proj, value_proj])
    prev_rim = from_behind(stacked[:, tokens - rim_rows :], "ctx", 1)
    extended = jnp.concatenate([prev_rim, stacked], axis=1).astype(jnp.float32)
    weights = [short_weights[:, offset, None, :] for offset in range(tap_count)]
    short_out = causal_taps(extended, weights, tokens, 1)
    product = (short_out[1] * short_out[2]).astype(jnp.bfloat16)
    cot_wide = cotangent.astype(jnp.float32)
    gate_grad = (cot_wide * short_out[0]).astype(jnp.bfloat16)
    filter_spec = receive_filter(filter_taps, dft_plan)
    prod_chan = lax.all_to_all(product.T, "ctx", split_axis=0, concat_axis=1, tiled=True)
    conv_chan, prod_spec = conv_forward(prod_chan, filter_spec, dft_plan)
    conv_tok = lax.all_to_all(conv_chan, "ctx", split_axis=1, concat_axis=0, tiled=True)
    grad_chan = lax.all_to_all(gate_grad.T, "ctx", split_axis=0, concat_axis=1, tiled=True)
    dconv_chan, dfilter_chan = conv_backward(
        grad_chan, filter_spec, prod_spec, dft_plan, grad_scale
    )
    dconv_tok = lax.all_to_all(dconv_chan, "ctx", split_axis=1, concat_axis=0, tiled=True)
    filter_grad = return_filter(dfilter_chan)
    conv_wide = conv_tok.T.astype(jnp.float32)
    dconv_wide = dconv_tok.T.astype(jnp.float32)
    gated = (short_out[0] * conv_wide).astype(jnp.bfloat16)
    token_grads = jnp.stack(
        [cot_wide * conv_wide, dconv_wide * short_out[2], dconv_wide * short_out[1]]
    )
    next_rim = from_behind(token_grads[:, :rim_rows], "ctx", -1)
    grad_ext = jnp.concatenate([token_grads, next_rim], axis=1)
    inputs_grad = reverse_taps(grad_ext, weights, tokens, 1).astype(jnp.bfloat16)
    weight_part = tap_grads(token_grads, extended, tap_count, tokens, 1)
    short_grad = lax.psum(weight_part, "ctx") * grad_scale
    results = (gated, inputs_grad[0], inputs_grad[1], inputs_grad[2])
    return (results[0], results[1], results[2], results[3], filter_grad, short_grad)


def solution(mesh):
    placed = (
        P("ctx", "tp"),
        P("ctx", "tp"),
        P("ctx", "tp"),
        P("ctx", "tp"),
        P("ctx", "tp"),
        P(None, None, "tp"),
    )
    return jax.shard_map(
        shards,
        mesh=mesh,
        in_specs=placed,
        out_specs=(
            P("ctx", "tp"),
            P("ctx", "tp"),
            P("ctx", "tp"),
            P("ctx", "tp"),
            P("ctx", "tp"),
            P(None, None, "tp"),
        ),
        check_vma=False,
    )
```

profile of v0, /device:TPU:256, one launch (start us, length us, event | category | flops | bytes accessed | tf_op | source)
XLA Modules:
  0.0 1284.4 jit_solution(9625832330967187007)
XLA Ops:
  4.9 3.4 collective-permute-start
  10.9 2.0 maximum_convert_fusion
  12.9 2.4 multiply_add_fusion
  17.2 17.1 %all-to-all-start.3 = ((bf16[128,8,128]{2,1,0:T(8,128)(2,1)}), bf16[128,8,128]{2,1,0:T(8,128)(2,1)S(1)}, u32[]{:S(2)}, u32[]{:S(2)}) async-start(bf16[128,8,128]{2,1,0:T(8,128)(2,1)} %fusion.92), calls=%async_computation.3 | async-start | bytes 524288 | tf_op jit(solution)/shard_map/all_to_all | solution.py:175
  34.3 2.0 copy.69
  36.4 18.0 %all-to-all-done.3 = bf16[128,8,128]{2,1,0:T(8,128)(2,1)S(1)} async-done(((bf16[128,8,128]{2,1,0:T(8,128)(2,1)}), bf16[128,8,128]{2,1,0:T(8,128)(2,1)S(1)}, u32[]{:S(2)}, u32[]{:S(2)}) %all-to-all-start.3) | async-done | bytes 262176 | tf_op jit(solution)/shard_map/all_to_all | solution.py:175
  54.4 8.1 all-to-all-start.1
  66.2 3.3 convolution_bitcast_fusion.1
  69.5 23.2 %all-to-all-done.1 = f32[128,8,128]{2,1,0:T(8,128)} async-done(((f32[128,8,128]{2,1,0:T(8,128)}), f32[128,8,128]{2,1,0:T(8,128)}, u32[]{:S(2)}, u32[]{:S(2)}) %all-to-all-start.1) | async-done | bytes 524320 | tf_op jit(solution)/shard_map/all_to_all | solution.py:110
  92.7 3.1 convolution_bitcast_fusion
  96.8 2.0 fusion.36
  98.8 2.0 fusion.30
  101.7 3.9 fusion.39
  108.0 28.0 %all_to_all.78 = bf16[8,128,128]{2,0,1:T(8,128)(2,1)S(1)} all-to-all(bf16[8,128,128]{2,0,1:T(8,128)(2,1)S(1)} %copy.84), channel_id=1, replica_groups=mesh['ctx'=128,'tp'=4] {'ctx'}, dimensions={1} | all-to-all | bytes 524288 | tf_op jit(solution)/shard_map/all_to_all | solution.py:179
  137.1 27.6 %all_to_all.79 = bf16[128,8,128]{2,1,0:T(8,128)(2,1)S(1)} all-to-all(bf16[128,8,128]{2,1,0:T(8,128)(2,1)S(1)} %get-tuple-element.44), channel_id=1, replica_groups=mesh['ctx'=128,'tp'=4] {'ctx'}, dimensions={0} | all-to-all | bytes 524288 | tf_op jit(solution)/shard_map/all_to_all | solution.py:172
  165.9 2.0 fusion.27
  168.7 3.6 fusion.42
  172.3 3.6 fusion.33
  175.9 2.0 multiply_subtract_fusion
  180.3 8.1 all-to-all-start.2
  188.3 2.9 fusion.81
  192.1 16.2 %all-to-all-done.2 = bf16[8,128,128]{2,0,1:T(8,128)(2,1)} async-done(((bf16[8,128,128]{2,0,1:T(8,128)(2,1)}), bf16[8,128,128]{2,0,1:T(8,128)(2,1)}, u32[]{:S(2)}, u32[]{:S(2)}) %all-to-all-start.2) | async-done | bytes 262176 | tf_op jit(solution)/shard_map/all_to_all | solution.py:174
  208.3 7.9 all-to-all-start.5
  216.3 2.0 fusion.84
  219.6 1.9 copy.85
  222.7 13.5 %all-to-all-done.5 = bf16[8,128,128]{2,0,1:T(8,128)(2,1)} async-done(((bf16[8,128,128]{2,0,1:T(8,128)(2,1)}), bf16[8,128,128]{2,0,1:T(8,128)(2,1)}, u32[]{:S(2)}, u32[]{:S(2)}) %all-to-all-start.5) | async-done | bytes 262176 | tf_op jit(solution)/shard_map/all_to_all | solution.py:116
  236.2 1.8 convert_bitcast_fusion
  238.8 2.0 copy.96
  240.9 1.7 copy.86
  242.6 2.2 pad_maximum_fusion
  244.9 5.2 multiply_reduce_fusion.2
  250.1 1029.7 %psum.7 = f32[3,3,1024]{2,0,1:T(4,128)S(1)} all-reduce(f32[3,3,1024]{2,0,1:T(4,128)S(1)} %pad_maximum_fusion.15), channel_id=1, replica_groups=mesh['ctx'=128,'tp'=4] {'ctx'}, use_global_device_ids=true, to_apply=%region_3.4 | all-reduce | flops 9216 | bytes 73728 | tf_op jit(solution)/shard_map/psum | solution.py:191
  (103 shorter events, 30.9 us)
Async XLA Ops:
  0.6 7.7 copy-start.30
  0.6 7.7 copy-start.22
  1.8 7.9 copy-start.11
  3.1 6.6 copy-start.12
  4.3 5.4 copy-start.13
  4.9 4.8 collective-permute-start
  8.3 4.5 copy-start.23
  8.4 4.5 copy-start.25
  8.6 6.7 copy-start.9
  15.3 1.2 copy-start
  17.2 37.2 %all-to-all-start.3 = ((bf16[128,8,128]{2,1,0:T(8,128)(2,1)}), bf16[128,8,128]{2,1,0:T(8,128)(2,1)S(1)}, u32[]{:S(2)}, u32[]{:S(2)}) async-start(bf16[128,8,128]{2,1,0:T(8,128)(2,1)} %fusion.92), calls=%async_computation.3 | async-start | bytes 524288 | tf_op jit(solution)/shard_map/all_to_all | solution.py:175
  54.4 8.4 copy-start.20
  54.4 38.3 %all-to-all-start.1 = ((f32[128,8,128]{2,1,0:T(8,128)}), f32[128,8,128]{2,1,0:T(8,128)}, u32[]{:S(2)}, u32[]{:S(2)}) async-start(f32[128,8,128]{2,1,0:T(8,128)} %bitcast.253), calls=%async_computation.1 | async-start | bytes 1048576 | tf_op jit(solution)/shard_map/all_to_all | solution.py:110
  92.7 3.1 copy-start.8
  95.8 1.0 copy-start.19
  100.7 1.0 copy-start.17
  105.9 30.1 %copy-start.1 = (f32[3,128,1024]{1,2,0:T(8,128)S(1)}, f32[3,128,1024]{1,2,0:T(8,128)}, u32[]{:S(2)}) copy-start(f32[3,128,1024]{1,2,0:T(8,128)} %copy-done) | copy-start | bytes 4718596
  107.8 56.8 %copy-start.15 = (f32[128,1,256]{0,2,1:T(8,128)S(1)}, f32[128,1,256]{0,2,1:T(8,128)}, u32[]{:S(2)}) copy-start(f32[128,1,256]{0,2,1:T(8,128)} %copy-done.14) | copy-start | bytes 393220
  177.9 10.4 copy-start.28
  180.3 36.0 %copy-start.10 = (bf16[128,1024]{0,1:T(8,128)(2,1)S(1)}, bf16[128,1024]{0,1:T(8,128)(2,1)}, u32[]{:S(2)}) copy-start(bf16[128,1024]{0,1:T(8,128)(2,1)} %copy-done.9) | copy-start | bytes 786436
  180.3 28.0 %all-to-all-start.2 = ((bf16[8,128,128]{2,0,1:T(8,128)(2,1)}), bf16[8,128,128]{2,0,1:T(8,128)(2,1)}, u32[]{:S(2)}, u32[]{:S(2)}) async-start(bf16[8,128,128]{2,0,1:T(8,128)(2,1)} %copy.76), calls=%async_computation.2 | async-start | bytes 524288 | tf_op jit(solution)/shard_map/all_to_all | solution.py:174
  208.3 27.9 %all-to-all-start.5 = ((bf16[8,128,128]{2,0,1:T(8,128)(2,1)}), bf16[8,128,128]{2,0,1:T(8,128)(2,1)}, u32[]{:S(2)}, u32[]{:S(2)}) async-start(bf16[8,128,128]{2,0,1:T(8,128)(2,1)} %copy.91), calls=%async_computation.5 | async-start | bytes 524288 | tf_op jit(solution)/shard_map/all_to_all | solution.py:116
  216.2 2.0 copy-start.2
  216.2 2.0 copy-start.4
  218.3 1.3 copy-start.6
  218.3 19.7 %copy-start.21 = (bf16[128,1024]{0,1:T(8,128)(2,1)S(1)}, bf16[128,1024]{0,1:T(8,128)(2,1)}, u32[]{:S(2)}) copy-start(bf16[128,1024]{0,1:T(8,128)(2,1)} %get-tuple-element.51) | copy-start | bytes 786436
  221.4 19.4 %collective-permute-start.1 = (f32[3,2,1024]{2,1,0:T(2,128)S(1)}, f32[3,2,1024]{2,1,0:T(2,128)S(1)}, u32[]{:S(2)}, u32[]{:S(2)}) collective-permute-start(f32[3,2,1024]{2,1,0:T(2,128)S(1)} %copy.85), channel_id=1, source_target_pairs={{4,0},{8,4},{12,8},{16,12},{20,16},{24,20},{28,24},{32,28},{36,32}... | collective-permute-start | bytes 73736 | tf_op jit(solution)/shard_map/ppermute | solution.py:11
  242.6 2.2 copy-start.3
  242.6 2.2 copy-start.5
  242.6 2.3 copy-start.7
  242.6 2.3 copy-start.24
  242.6 2.3 copy-start.26
  (5 other events, 4.5 us)
where the time goes:
time: 1290 us; the launch traced here: 1280 us
  blocking collectives  1090 us (84%)
  waiting for transfers between devices  72 us (6%)
  starting transfers between devices  45.9 us (4%)
  matrix products  29.9 us (2%)
  other arithmetic  26.8 us (2%)
  local copies, waits for them, and re-layouts  23.2 us (2%)
    psum x1, blocking collectives, shards(): short_grad = lax.psum(weight_part, 'ctx') * grad_scale  1030 us
    dot_general x12, matrix products, contract(): jnp.einsum(form, left, right, precision=lax.Precision.HIGHEST, preferred_...  29.9 us
    all_to_all x1, blocking collectives, shards(): lax.all_to_all(dconv_chan, 'ctx', split_axis=1, concat_axis=0, tiled=True)  28 us
    all_to_all x1, blocking collectives, shards(): lax.all_to_all(product.T, 'ctx', split_axis=0, concat_axis=1, tiled=True)  27.6 us
  transfers between devices with their start and end apart: 6, of which 5 were waited for; matrix products, arithmetic and copies ran while one was open for 2% of the time, Pallas kernels for 0%

commit v1 on v0

--- a/solution.py
+++ b/solution.py
@@ -3,6 +3,10 @@
 import jax.numpy as jnp
 from jax import lax
 from jax.sharding import PartitionSpec as P
+
+
+def expand_space(page):
+    return jnp.sum(lax.all_gather(page, axis_name="ctx"), 0)
 
 
 def from_behind(array, axis, by):
@@ -188,7 +192,7 @@
     grad_ext = jnp.concatenate([token_grads, next_rim], axis=1)
     inputs_grad = reverse_taps(grad_ext, weights, tokens, 1).astype(jnp.bfloat16)
     weight_part = tap_grads(token_grads, extended, tap_count, tokens, 1)
-    short_grad = lax.psum(weight_part, "ctx") * grad_scale
+    short_grad = expand_space(weight_part) * grad_scale
     results = (gated, inputs_grad[0], inputs_grad[1], inputs_grad[2])
     return (results[0], results[1], results[2], results[3], filter_grad, short_grad)
 

time: 1290 us -> 1220 us (0.946)
  the two profiles are of different devices: /device:TPU:256 before, /device:TPU:0 now
where the time goes in v1:
time: 1220 us
  waiting for transfers between devices  998 us (82%)
  blocking collectives  83.1 us (7%)
  starting transfers between devices  45.1 us (4%)
  matrix products  29.9 us (2%)
  other arithmetic  26.8 us (2%)
  local copies, waits for them, and re-layouts  20.3 us (2%)
  between operations  14.8 us (1%)
    all_gather x1, waiting for transfers between devices, expand_space(): return jnp.sum(lax.all_gather(page, axis_name='ctx'), 0)  932 us
    dot_general x12, matrix products, contract(): jnp.einsum(form, left, right, precision=lax.Precision.HIGHEST, preferred_...  29.9 us
    all_to_all x1, blocking collectives, shards(): lax.all_to_all(dconv_chan, 'ctx', split_axis=1, concat_axis=0, tiled=True)  28 us
    all_to_all x1, blocking collectives, shards(): lax.all_to_all(product.T, 'ctx', split_axis=0, concat_axis=1, tiled=True)  27.6 us
    all_to_all x1, blocking collectives, shards(): lax.all_to_all(conv_chan, 'ctx', split_axis=1, concat_axis=0, tiled=True)  27.6 us
  transfers between devices with their start and end apart: 6, of which 6 were waited for; matrix products, arithmetic and copies ran while one was open for 1% of the time, Pallas kernels for 0%

profile of v1, /device:TPU:0, one launch (start us, length us, event | category | flops | bytes accessed | tf_op | source)
XLA Modules:
  0.0 1218.4 jit_solution(12358425093221357213)
XLA Ops:
  15.3 2.0 maximum_convert_fusion
  17.3 2.4 multiply_add_fusion
  21.6 17.4 %all-to-all-start.3 = ((bf16[128,8,128]{2,1,0:T(8,128)(2,1)}), bf16[128,8,128]{2,1,0:T(8,128)(2,1)S(1)}, u32[]{:S(2)}, u32[]{:S(2)}) async-start(bf16[128,8,128]{2,1,0:T(8,128)(2,1)} %fusion.92), calls=%async_computation.3 | async-start | bytes 524288 | tf_op jit(solution)/shard_map/all_to_all | solution.py:179
  39.0 2.0 copy.68
  41.1 18.0 %all-to-all-done.3 = bf16[128,8,128]{2,1,0:T(8,128)(2,1)S(1)} async-done(((bf16[128,8,128]{2,1,0:T(8,128)(2,1)}), bf16[128,8,128]{2,1,0:T(8,128)(2,1)S(1)}, u32[]{:S(2)}, u32[]{:S(2)}) %all-to-all-start.3) | async-done | bytes 262176 | tf_op jit(solution)/shard_map/all_to_all | solution.py:179
  59.1 7.9 all-to-all-start.1
  71.0 3.3 convolution_bitcast_fusion.1
  74.3 23.2 %all-to-all-done.1 = f32[128,8,128]{2,1,0:T(8,128)} async-done(((f32[128,8,128]{2,1,0:T(8,128)}), f32[128,8,128]{2,1,0:T(8,128)}, u32[]{:S(2)}, u32[]{:S(2)}) %all-to-all-start.1) | async-done | bytes 524320 | tf_op jit(solution)/shard_map/all_to_all | solution.py:114
  97.4 3.1 convolution_bitcast_fusion
  101.5 1.9 fusion.36
  103.5 2.0 fusion.30
  106.4 3.8 fusion.39
  112.7 28.0 %all_to_all.78 = bf16[8,128,128]{2,0,1:T(8,128)(2,1)S(1)} all-to-all(bf16[8,128,128]{2,0,1:T(8,128)(2,1)S(1)} %copy.83), channel_id=1, replica_groups=mesh['ctx'=128,'tp'=4] {'ctx'}, dimensions={1} | all-to-all | bytes 524288 | tf_op jit(solution)/shard_map/all_to_all | solution.py:183
  140.8 27.6 %all_to_all.79 = bf16[128,8,128]{2,1,0:T(8,128)(2,1)S(1)} all-to-all(bf16[128,8,128]{2,1,0:T(8,128)(2,1)S(1)} %get-tuple-element.44), channel_id=1, replica_groups=mesh['ctx'=128,'tp'=4] {'ctx'}, dimensions={0} | all-to-all | bytes 524288 | tf_op jit(solution)/shard_map/all_to_all | solution.py:176
  169.6 2.0 fusion.27
  172.4 3.6 fusion.42
  176.0 3.6 fusion.33
  179.6 2.0 multiply_subtract_fusion
  181.6 1.4 fusion.75
  183.2 27.6 %all_to_all.80 = bf16[8,128,128]{2,0,1:T(8,128)(2,1)S(1)} all-to-all(bf16[8,128,128]{2,0,1:T(8,128)(2,1)S(1)} %copy.75), channel_id=1, replica_groups=mesh['ctx'=128,'tp'=4] {'ctx'}, dimensions={1} | all-to-all | bytes 524288 | tf_op jit(solution)/shard_map/all_to_all | solution.py:178
  210.9 1.3 pad_maximum_fusion.4
  212.2 1.9 copy.84
  214.1 1.3 collective-permute-start.1
  215.4 4.4 collective-permute-done.1
  219.8 1.7 copy.85
  221.5 2.2 pad_maximum_fusion
  223.8 5.2 multiply_reduce_fusion.2
  229.8 3.0 fusion.81
  233.6 17.0 %all-to-all-start.5 = ((bf16[8,128,128]{2,0,1:T(8,128)(2,1)}), bf16[8,128,128]{2,0,1:T(8,128)(2,1)S(1)}, u32[]{:S(2)}, u32[]{:S(2)}) async-start(bf16[8,128,128]{2,0,1:T(8,128)(2,1)} %copy.90), calls=%async_computation.5 | async-start | bytes 524288 | tf_op jit(solution)/shard_map/all_to_all | solution.py:120
  251.5 19.1 %all-to-all-done.5 = bf16[8,128,128]{2,0,1:T(8,128)(2,1)S(1)} async-done(((bf16[8,128,128]{2,0,1:T(8,128)(2,1)}), bf16[8,128,128]{2,0,1:T(8,128)(2,1)S(1)}, u32[]{:S(2)}, u32[]{:S(2)}) %all-to-all-start.5) | async-done | bytes 262176 | tf_op jit(solution)/shard_map/all_to_all | solution.py:120
  274.3 932.4 %all-gather.3.cloned.1.call-done = f32[384,3,1024]{2,1,0:T(4,128)} async-done(((f32[3,3,1024]{2,1,0:T(4,128)}), f32[384,3,1024]{2,1,0:T(4,128)}) %all-gather.3.cloned.1.call-update) | async-done | bytes 4718608 | tf_op jit(solution)/shard_map/all_gather | solution.py:9
  1206.7 4.0 reduce_sum.39
  (106 shorter events, 27.4 us)
Async XLA Ops:
  7.2 5.5 copy-start.29
  7.2 5.6 copy-start.22
  8.4 5.7 copy-start.12
  9.6 4.5 copy-start.13
  10.8 3.3 copy-start.14
  11.4 2.7 collective-permute-start
  12.8 4.5 copy-start.23
  12.8 4.5 copy-start.25
  13.0 6.7 copy-start.10
  19.7 1.2 copy-start
  21.6 37.4 %all-to-all-start.3 = ((bf16[128,8,128]{2,1,0:T(8,128)(2,1)}), bf16[128,8,128]{2,1,0:T(8,128)(2,1)S(1)}, u32[]{:S(2)}, u32[]{:S(2)}) async-start(bf16[128,8,128]{2,1,0:T(8,128)(2,1)} %fusion.92), calls=%async_computation.3 | async-start | bytes 524288 | tf_op jit(solution)/shard_map/all_to_all | solution.py:179
  59.1 8.4 copy-start.21
  59.1 38.3 %all-to-all-start.1 = ((f32[128,8,128]{2,1,0:T(8,128)}), f32[128,8,128]{2,1,0:T(8,128)}, u32[]{:S(2)}, u32[]{:S(2)}) async-start(f32[128,8,128]{2,1,0:T(8,128)} %bitcast.252), calls=%async_computation.1 | async-start | bytes 1048576 | tf_op jit(solution)/shard_map/all_to_all | solution.py:114
  67.0 1139.6 %all-gather.3.cloned.1.call-start = ((), (), s32[]{:S(2)}) async-start(), calls=%async_computation.6 | async-start | bytes 6340608 | tf_op jit(solution)/shard_map/all_gather | solution.py:9
  97.4 3.1 copy-start.8
  100.5 1.0 copy-start.20
  105.4 1.0 copy-start.18
  110.2 1.0 copy-start.28
  110.5 30.1 %copy-start.1 = (f32[3,128,1024]{1,2,0:T(8,128)S(1)}, f32[3,128,1024]{1,2,0:T(8,128)}, u32[]{:S(2)}) copy-start(f32[3,128,1024]{1,2,0:T(8,128)} %copy-done) | copy-start | bytes 4718596
  112.5 55.9 %copy-start.16 = (f32[128,1,256]{0,2,1:T(8,128)S(1)}, f32[128,1,256]{0,2,1:T(8,128)}, u32[]{:S(2)}) copy-start(f32[128,1,256]{0,2,1:T(8,128)} %copy-done.15) | copy-start | bytes 393220
  140.7 70.1 %copy-start.2 = (f32[1,128,1024]{1,2,0:T(8,128)}, f32[1,128,1024]{1,2,0:T(8,128)S(1)}, u32[]{:S(2)}) copy-start(f32[1,128,1024]{1,2,0:T(8,128)S(1)} %get-tuple-element.41) | copy-start | bytes 1572868
  140.8 70.1 %copy-start.4 = (f32[1,128,1024]{1,2,0:T(8,128)}, f32[1,128,1024]{1,2,0:T(8,128)S(1)}, u32[]{:S(2)}) copy-start(f32[1,128,1024]{1,2,0:T(8,128)S(1)} %get-tuple-element.42) | copy-start | bytes 1572868
  181.6 29.2 %copy-start.11 = (bf16[128,1024]{0,1:T(8,128)(2,1)S(1)}, bf16[128,1024]{0,1:T(8,128)(2,1)}, u32[]{:S(2)}) copy-start(bf16[128,1024]{0,1:T(8,128)(2,1)} %copy-done.10) | copy-start | bytes 786436
  210.9 1.3 copy-start.6
  214.1 5.7 collective-permute-start.1
  221.5 2.2 copy-start.3
  221.5 2.2 copy-start.5
  221.5 2.3 copy-start.7
  221.5 2.3 copy-start.24
  221.5 2.3 copy-start.26
  232.7 38.9 %copy-start.9 = (bf16[3,128,1024]{1,2,0:T(8,128)(2,1)S(1)}, bf16[3,128,1024]{1,2,0:T(8,128)(2,1)}, u32[]{:S(2)}) copy-start(bf16[3,128,1024]{1,2,0:T(8,128)(2,1)} %get-tuple-element.43) | copy-start | bytes 2359300
  233.6 37.0 %all-to-all-start.5 = ((bf16[8,128,128]{2,0,1:T(8,128)(2,1)}), bf16[8,128,128]{2,0,1:T(8,128)(2,1)S(1)}, u32[]{:S(2)}, u32[]{:S(2)}) async-start(bf16[8,128,128]{2,0,1:T(8,128)(2,1)} %copy.90), calls=%async_computation.5 | async-start | bytes 524288 | tf_op jit(solution)/shard_map/all_to_all | solution.py:120
  (4 other events, 3.6 us)
Sparse Core Ops, SparseCore 0:
  229.9 976.7 all-gather.2
